TPU v7x, 32 devices: a whole 2x2x4 slice. The times are simulated.
32 devices in a mesh: outer: 8 (over y, x, core), inner: 4 (over z).
Axes of the slice: x: 2, y: 2, z: 4, core: 2. Of those that a mesh axis runs over, the one named last changes fastest.
Arguments:
- queries: bfloat16 [4096, 768], P(('outer', 'inner')), may hold values from -5.5 to 5.5
- keys: bfloat16 [4096, 128], P(('outer', 'inner')), may hold values from -5.5 to 5.5
- values: bfloat16 [4096, 128], P(('outer', 'inner')), may hold values from -6 to 6
- grad_out: bfloat16 [4096, 768], P(('outer', 'inner')), may hold values from -96 to 96
- span_slot: int32 [64], replicated, may hold values from 0 to 63, as said below
Outputs:
- grad_queries: bfloat16 [4096, 768], P(('outer', 'inner'))
- grad_keys: bfloat16 [4096, 128], P(('outer', 'inner'))
- grad_values: bfloat16 [4096, 128], P(('outer', 'inner'))
Inputs may be any that keep to these rules, and one draw needn't show every extreme that they name: `span_slot`: slots 2 d and 2 d + 1 hold spans c and 63 - c for some c below 32; every span is held once.
All inputs are finite; a program needn't handle non-finite values.
Results may differ from a plain program's by a relative error of at most 0.0074.
Values may be sent and summed in bfloat16 or wider, within the bound.
A program may use at most 128 MiB of HBM per device.

v0:
```python
import math

import jax
import jax.numpy as jnp
from jax import lax
from jax.sharding import PartitionSpec as P

NEG_FILL = -1e30


def slot_positions(slots, span_len):
    offsets = jnp.arange(span_len, dtype=jnp.int32)
    return (slots[:, None] * span_len + offsets[None, :]).reshape(-1)


def grad_terms(q_rows, do_rows, k_blk, v_blk, live, lse, delta, scale):
    scores = jnp.dot(q_rows, k_blk.T, preferred_element_type=jnp.float32) * scale
    probs = jnp.where(live, jnp.exp(scores - lse[:, None]), 0.0)
    dprobs = jnp.dot(do_rows, v_blk.T, preferred_element_type=jnp.float32)
    dscores = (probs * (dprobs - delta[:, None]) * scale).astype(jnp.bfloat16)
    return (probs, dscores)


def local(queries, keys, values, grad_out, span_slot):
    tok_rows = keys.shape[0]
    span_len = tok_rows // 2
    head_dim = keys.shape[1]
    group = queries.shape[1] // head_dim
    scale = 1.0 / math.sqrt(head_dim)
    keys_all, values_all = (
        lax.all_gather(keys, ("outer", "inner"), axis=0, tiled=True),
        lax.all_gather(values, ("outer", "inner"), axis=0, tiled=True),
    )
    total_rows = keys_all.shape[0]
    key_pos = slot_positions(span_slot, span_len)
    linear = lax.axis_index(("outer", "inner"))
    own_slots = lax.dynamic_slice_in_dim(span_slot, 2 * linear, 2, 0)
    q_pos = jnp.repeat(slot_positions(own_slots, span_len), group)
    q_rows = queries.reshape(tok_rows * group, head_dim)
    do_rows = grad_out.reshape(tok_rows * group, head_dim)
    width = q_rows.shape[0]
    key_block = math.gcd(total_rows, 512)
    contract = (((0,), (0,)), ((), ()))

    def stats_step(index, carry):
        top, total, weighted = carry
        first = index * key_block
        k_blk = lax.dynamic_slice_in_dim(keys_all, first, key_block, 0)
        v_blk = lax.dynamic_slice_in_dim(values_all, first, key_block, 0)
        k_pos = lax.dynamic_slice_in_dim(key_pos, first, key_block, 0)
        live = q_pos[:, None] >= k_pos[None, :]
        scores = jnp.where(
            live, jnp.dot(q_rows, k_blk.T, preferred_element_type=jnp.float32) * scale, NEG_FILL
        )
        dprobs = jnp.dot(do_rows, v_blk.T, preferred_element_type=jnp.float32)
        new_top = jnp.maximum(top, jnp.max(scores, axis=1))
        shrink = jnp.exp(top - new_top)
        expo = jnp.where(live, jnp.exp(scores - new_top[:, None]), 0.0)
        return (
            new_top,
            total * shrink + jnp.sum(expo, axis=1),
            weighted * shrink + jnp.sum(expo * dprobs, axis=1),
        )

    start_stats = (
        jnp.full((width,), NEG_FILL, jnp.float32),
        jnp.zeros((width,), jnp.float32),
        jnp.zeros((width,), jnp.float32),
    )
    top, total, weighted = lax.fori_loop(0, total_rows // key_block, stats_step, start_stats)
    lse = top + jnp.log(total)
    delta = weighted / total

    def block_terms(first, size):
        k_blk = lax.dynamic_slice_in_dim(keys_all, first, size, 0)
        v_blk = lax.dynamic_slice_in_dim(values_all, first, size, 0)
        k_pos = lax.dynamic_slice_in_dim(key_pos, first, size, 0)
        live = q_pos[:, None] >= k_pos[None, :]
        probs, dscores = grad_terms(q_rows, do_rows, k_blk, v_blk, live, lse, delta, scale)
        dkey = lax.dot_general(dscores, q_rows, contract, preferred_element_type=jnp.float32)
        dval = lax.dot_general(
            probs.astype(jnp.bfloat16), do_rows, contract, preferred_element_type=jnp.float32
        )
        return (k_blk, dscores, jnp.concatenate([dkey, dval], axis=1))

    def joint_step(index, carry):
        acc, terms = carry
        first = index * key_block
        k_blk, dscores, piece = block_terms(first, key_block)
        acc = acc + jnp.dot(dscores, k_blk, preferred_element_type=jnp.float32)
        return (acc, lax.dynamic_update_slice_in_dim(terms, piece, first, 0))

    start_joint = (
        jnp.zeros((width, head_dim), jnp.float32),
        jnp.zeros((total_rows, 2 * head_dim), jnp.float32),
    )
    dq_acc, all_terms = lax.fori_loop(0, total_rows // key_block, joint_step, start_joint)
    summed = lax.psum_scatter(all_terms, ("outer", "inner"), scatter_dimension=0, tiled=True)
    grad_queries = dq_acc.astype(jnp.bfloat16).reshape(tok_rows, group * head_dim)
    grad_keys = summed[:, :head_dim].astype(jnp.bfloat16)
    grad_values = summed[:, head_dim:].astype(jnp.bfloat16)
    return (grad_queries, grad_keys, grad_values)


def solution(mesh):
    placed = (
        P(("outer", "inner"), None),
        P(("outer", "inner"), None),
        P(("outer", "inner"), None),
        P(("outer", "inner"), None),
        P(),
    )
    return jax.shard_map(
        local,
        mesh=mesh,
        in_specs=placed,
        out_specs=(
            P(("outer", "inner"), None),
            P(("outer", "inner"), None),
            P(("outer", "inner"), None),
        ),
        check_vma=False,
    )
```

profile of v0, /device:TPU:0, one launch (start us, length us, event | category | flops | bytes accessed | tf_op | source)
XLA Modules:
  0.0 358.0 jit_solution(1580818840185862535)
XLA Ops:
  7.2 0.7 all-gather.3.cloned.1.call-update
  7.9 0.7 all-gather.5.cloned.1.call-update
  8.7 0.7 dynamic-slice_multiply_fusion
  9.6 0.7 broadcast_multiply_fusion
  10.4 1.1 reshape.34
  11.6 1.1 reshape.35
  12.7 54.8 %all-gather.3.cloned.1.call-done = bf16[4096,128]{1,0:T(8,128)(2,1)} async-done(((bf16[128,128]{1,0:T(8,128)(2,1)}), bf16[4096,128]{1,0:T(8,128)(2,1)}) %all-gather.3.cloned.1.call-update) | async-done | bytes 1048592 | tf_op jit(solution)/shard_map/all_gather | solution.py:31
  67.5 55.7 %all-gather.5.cloned.1.call-done = bf16[4096,128]{1,0:T(8,128)(2,1)} async-done(((bf16[128,128]{1,0:T(8,128)(2,1)}), bf16[4096,128]{1,0:T(8,128)(2,1)}) %all-gather.5.cloned.1.call-update) | async-done | bytes 1048592 | tf_op jit(solution)/shard_map/all_gather | solution.py:32
  123.2 27.3 %while.34 = (s32[]{:T(128)}, f32[768]{0:T(1024)S(1)}, f32[768]{0:T(1024)S(1)}, f32[768]{0:T(1024)S(1)}, s32[4096]{0:T(1024)S(1)}, /*index=5*/bf16[4096,128]{1,0:...) while((s32[]{:T(128)}, f32[768]{0:T(1024)S(1)}, ...), condition=%wide.region_4.5_spmd.clone, body=%wide.region_0.4_spmd.clone.sunk | while | flops 206443776 | bytes 5458642 | solution.py:70
  123.5 1.3 fusion.57
  124.8 1.4 fusion.58
  126.9 1.3 fusion.57
  128.3 1.4 fusion.58
  130.4 1.3 fusion.57
  131.7 1.4 fusion.58
  133.8 1.3 fusion.57
  135.1 1.4 fusion.58
  137.2 1.3 fusion.57
  138.5 1.4 fusion.58
  140.6 1.3 fusion.57
  141.9 1.4 fusion.58
  144.0 1.3 fusion.57
  145.3 1.4 fusion.58
  147.5 1.3 fusion.57
  148.8 1.4 fusion.58
  150.6 2.2 broadcast_in_dim.54.clone
  152.8 50.2 %while.35 = (s32[]{:T(128)}, f32[768,128]{1,0:T(8,128)S(1)}, f32[4096,256]{1,0:T(8,128)}, s32[4096]{0:T(1024)S(1)}, bf16[4096,128]{1,0:T(8,128)(2,1)}, /*index=5...) while((s32[]{:T(128)}, f32[768,128]{1,0:T(8,128)S(1)}, ...), condition=%wide.region_6.7_spmd.clone, body=%wide.region_5.6_spmd.clone.sunk | while | flops 507183104 | bytes 12739297 | solution.py:97
  153.1 1.4 bitcast_select_fusion.2
  154.9 1.3 fusion.71
  156.6 1.4 convolution_add_fusion.2
  158.2 0.8 constant_dynamic-update-slice_fusion.2
  159.4 1.4 bitcast_select_fusion.2
  161.2 1.3 fusion.71
  162.4 0.4 fusion.73
  162.9 1.4 convolution_add_fusion.2
  164.5 0.8 constant_dynamic-update-slice_fusion.2
  165.6 1.4 bitcast_select_fusion.2
  167.4 1.3 fusion.71
  169.1 1.4 convolution_add_fusion.2
  170.8 0.8 constant_dynamic-update-slice_fusion.2
  171.9 1.4 bitcast_select_fusion.2
  173.7 1.3 fusion.71
  175.4 1.4 convolution_add_fusion.2
  177.1 0.8 constant_dynamic-update-slice_fusion.2
  178.2 1.4 bitcast_select_fusion.2
  180.0 1.3 fusion.71
  181.7 1.4 convolution_add_fusion.2
  183.3 0.8 constant_dynamic-update-slice_fusion.2
  184.5 1.4 bitcast_select_fusion.2
  186.3 1.3 fusion.71
  188.0 1.4 convolution_add_fusion.2
  189.6 0.9 constant_dynamic-update-slice_fusion.2
  190.8 1.4 bitcast_select_fusion.2
  192.6 1.3 fusion.71
  194.2 1.4 convolution_add_fusion.2
  195.9 0.8 constant_dynamic-update-slice_fusion.2
  197.0 1.4 bitcast_select_fusion.2
  198.8 1.3 fusion.71
  200.5 1.4 convolution_add_fusion.2
  202.2 0.8 constant_dynamic-update-slice_fusion.2
  203.1 0.9 reshape.36
  203.9 146.0 %reduce-scatter.2.cloned.1.call-done = f32[128,256]{1,0:T(8,128)} async-done(((f32[4096,256]{1,0:T(8,128)}), f32[128,256]{1,0:T(8,128)}) %reduce-scatter.2.cloned.1.call-update) | async-done | bytes 131088 | tf_op jit(solution)/shard_map/reduce_scatter | solution.py:98
  349.9 0.9 convert.4
  350.8 0.6 fusion.23
  (125 shorter events, 15.7 us)
Async XLA Ops:
  7.2 60.3 %all-gather.3.cloned.1.call-start = ((), (), s32[]{:S(2)}) async-start(), calls=%async_computation.1 | async-start | bytes 1081344 | tf_op jit(solution)/shard_map/all_gather | solution.py:31
  7.9 115.3 %all-gather.5.cloned.1.call-start = ((), (), s32[]{:S(2)}) async-start(), calls=%async_computation.2 | async-start | bytes 1081344 | tf_op jit(solution)/shard_map/all_gather | solution.py:32
  8.6 341.2 %reduce-scatter.2.cloned.1.call-start = ((), (), s32[]{:S(2)}) async-start(), calls=%async_computation.3 | async-start | bytes 4325376 | tf_op jit(solution)/shard_map/reduce_scatter | solution.py:98
Sparse Core Ops, SparseCore 0:
  11.0 56.4 all-gather.2
  70.5 52.7 all-gather.4
  203.1 146.7 reduce-scatter.1
where the time goes:
time: 359 us; the launch traced here: 358 us
  waiting for transfers between devices  258 us (72%)
  matrix products  60.4 us (17%)
  local copies, waits for them, and re-layouts  19 us (5%)
  between operations  13.8 us (4%)
  other arithmetic  5.61 us (2%)
    reduce_scatter x1, waiting for transfers between devices, local(): lax.psum_scatter(all_terms, ('outer', 'inner'), scatter_dimension=0, tile...  146 us
    all_gather x1, waiting for transfers between devices, local(): lax.all_gather(values, ('outer', 'inner'), axis=0, tiled=True)  55.7 us
    all_gather x1, waiting for transfers between devices, local(): lax.all_gather(keys, ('outer', 'inner'), axis=0, tiled=True)  54.8 us
    dot_general x8, matrix products, stats_step(): dprobs = jnp.dot(do_rows, v_blk.T, preferred_element_type=jnp.float32)  11.2 us
    dot_general x8, matrix products, grad_terms(): jnp.dot(q_rows, k_blk.T, preferred_element_type=jnp.float32) * scale  11.2 us
    dot_general x8, matrix products, joint_step(): acc = acc + jnp.dot(dscores, k_blk, preferred_element_type=jnp.float32)  11.2 us
    dot_general x8, matrix products, stats_step(): jnp.dot(q_rows, k_blk.T, preferred_element_type=jnp.float32) * scale  10.4 us
    dot_general x8, matrix products, grad_terms(): dprobs = jnp.dot(do_rows, v_blk.T, preferred_element_type=jnp.float32)  10.2 us
  transfers between devices with their start and end apart: 3, of which 3 were waited for; matrix products, arithmetic and copies ran while one was open for 1% of the time, Pallas kernels for 0%

commit v1 on v0

v1 whole, which is shorter than its diff:
```python
import functools
import math

import jax
import jax.numpy as jnp
import numpy as np
from jax import lax
from jax.experimental import pallas as pl
from jax.experimental.pallas import tpu as pltpu
from jax.sharding import PartitionSpec as P

NEG_FILL = -1e30
LOG2E = math.log2(math.e)
MIB = 1024 * 1024
MESH = pl.DeviceIdType.MESH


def bits_of(outer, inner):
    near = [("inner", b) for b in range(inner.bit_length() - 1)]
    chips = [("outer", b) for b in range(1, outer.bit_length() - 1)]
    core = [("outer", 0)]
    return near + chips + core, near + chips[::-1] + core


def place_of(order, o, i):
    place = 0
    for at, (axis, b) in enumerate(order):
        place = place + (((o if axis == "outer" else i) // 2**b) % 2) * 2**at
    return place


def partner_of(axis, b, o, i):
    if axis == "outer":
        return (o + (1 - 2 * ((o // 2**b) % 2)) * 2**b, i)
    return (o, i + (1 - 2 * ((i // 2**b) % 2)) * 2**b)


def greet(order, o, i):
    barrier = pltpu.get_barrier_semaphore()
    for axis, b in order:
        pl.semaphore_signal(barrier, inc=1, device_id=partner_of(axis, b, o, i), device_id_type=MESH)
    pl.semaphore_wait(barrier, len(order))


def gather_kernel(orders, k_in, v_in, k_out, v_out, send, recv):
    o, i = lax.axis_index("outer"), lax.axis_index("inner")
    rows = k_in.shape[0]
    steps = len(orders[0])
    greet(orders[0], o, i)
    places = [place_of(order, o, i) for order in orders]
    for src, out, place in ((k_in, k_out, places[0]), (v_in, v_out, places[1])):
        out[pl.ds(pl.multiple_of(place * rows, rows), rows), :] = src[...]
    copies = {}

    def begin(a, step):
        out = (k_out, v_out)[a]
        size = rows * 2**step
        part = out.at[pl.ds(pl.multiple_of((places[a] // 2**step) * size, size), size), :]
        axis, b = orders[a][step]
        copies[a, step] = pltpu.make_async_remote_copy(
            src_ref=part, dst_ref=part, send_sem=send.at[a, step], recv_sem=recv.at[a, step],
            device_id=partner_of(axis, b, o, i), device_id_type=MESH)
        copies[a, step].start()

    for a in (0, 1):
        begin(a, 0)
    for step in range(steps):
        for a in (0, 1):
            copies[a, step].wait_recv()
            if step + 1 < steps:
                begin(a, step + 1)
    for copy in copies.values():
        copy.wait_send()


def scatter_kernel(orders, k_in, v_in, k_out, v_out, k_acc, v_acc, k_got, v_got, send, recv):
    o, i = lax.axis_index("outer"), lax.axis_index("inner")
    rows = k_out.shape[0]
    steps = len(orders[0])
    half = 2 ** (steps - 1)
    greet(orders[0], o, i)
    places = [place_of(order, o, i) for order in orders]
    ins, outs, accs, gots = (k_in, v_in), (k_out, v_out), (k_acc, v_acc), (k_got, v_got)
    copies = {}

    def spot(place, step, wrap):
        size = rows * 2**step
        return pl.ds(pl.multiple_of(((place % wrap) // 2**step) * size, size), size)

    def begin(a, step):
        place, size = places[a], rows * 2**step
        theirs = place + (1 - 2 * ((place // 2**step) % 2)) * 2**step
        axis, b = orders[a][step]
        src = ins[a].at[spot(theirs, step, 2 * half), :] if step == steps - 1 else accs[a].at[spot(theirs, step, half), :]
        copies[a, step] = pltpu.make_async_remote_copy(
            src_ref=src, dst_ref=gots[a].at[pl.ds(size, size), :],
            send_sem=send.at[a, step], recv_sem=recv.at[a, step],
            device_id=partner_of(axis, b, o, i), device_id_type=MESH)
        copies[a, step].start()

    for a in (0, 1):
        begin(a, steps - 1)
    for step in range(steps - 1, -1, -1):
        size = rows * 2**step
        for a in (0, 1):
            copies[a, step].wait_recv()
            mine = ins[a][spot(places[a], step, 2 * half), :] if step == steps - 1 else accs[a][spot(places[a], step, half), :]
            total = mine.astype(jnp.float32) + gots[a][pl.ds(size, size), :].astype(jnp.float32)
            if step:
                accs[a][spot(places[a], step, half), :] = total.astype(jnp.bfloat16)
                begin(a, step - 1)
            else:
                outs[a][...] = total.astype(jnp.bfloat16)
    for copy in copies.values():
        copy.wait_send()


def attend_kernel(inner, blk_spans, slots, tab_k, tab_v, q_ref, do_ref, k_ref, v_ref,
                  dq_ref, dk_ref, dv_ref, at_k, at_v, ks, vs, dks, dvs):
    spans = slots.shape[0]
    span = q_ref.shape[0] // 2
    hd = k_ref.shape[1]
    group = q_ref.shape[1] // hd
    blk = blk_spans * span
    scale = 1.0 / math.sqrt(hd)
    f32 = jnp.float32
    linear = lax.axis_index("outer") * inner + lax.axis_index("inner")

    def note(j, _):
        s = slots[j]
        at_k[s] = tab_k[j]
        at_v[s] = tab_v[j]
        return 0

    lax.fori_loop(0, spans, note, 0)
    tops = [slots[2 * linear], slots[2 * linear + 1]]
    used = (tops[1] // blk_spans + 1) * blk_spans

    def sort(s, _):
        to = pl.ds(pl.multiple_of(s * span, span), span)
        ks[to, :] = k_ref[pl.ds(pl.multiple_of(at_k[s] * span, span), span), :]
        vs[to, :] = v_ref[pl.ds(pl.multiple_of(at_v[s] * span, span), span), :]
        return 0

    lax.fori_loop(0, used, sort, 0)
    nt = (((1,), (1,)), ((), ()))
    tn = (((0,), (0,)), ((), ()))
    width = group * span

    for g in (1, 0):
        rows = slice(g * span, (g + 1) * span)
        q = jnp.concatenate([q_ref[rows, h * hd:(h + 1) * hd] for h in range(group)], axis=0)
        do = jnp.concatenate([do_ref[rows, h * hd:(h + 1) * hd] for h in range(group)], axis=0)
        last = tops[g] // blk_spans
        lane = lax.broadcasted_iota(jnp.int32, (blk, width), 1) % span
        low = lax.broadcasted_iota(jnp.int32, (blk, width), 0)

        def load(n):
            at = pl.ds(pl.multiple_of(n * blk, blk), blk)
            return at, ks[at, :], vs[at, :]

        def logits(k, n, masked):
            t = lax.dot_general(k, q, nt, preferred_element_type=f32) * (scale * LOG2E)
            if masked:
                t = jnp.where(low + n * blk <= lane + tops[g] * span, t, NEG_FILL)
            return t

        def stats(n, carry, masked):
            top, total, weighted = carry
            _, k, v = load(n)
            t = logits(k, n, masked)
            dp = lax.dot_general(v, do, nt, preferred_element_type=f32)
            new = jnp.maximum(top, jnp.max(t, axis=0, keepdims=True))
            shrink = jnp.exp2(top - new)
            e = jnp.exp2(t - new)
            return (new, total * shrink + jnp.sum(e, axis=0, keepdims=True),
                    weighted * shrink + jnp.sum(e * dp, axis=0, keepdims=True))

        carry = (jnp.full((1, width), NEG_FILL, f32), jnp.zeros((1, width), f32), jnp.zeros((1, width), f32))
        carry = lax.fori_loop(0, last, functools.partial(stats, masked=False), carry)
        top, total, weighted = stats(last, carry, True)
        lse = top + jnp.log2(total)
        delta = weighted / total

        def grads(n, dq, masked):
            at, k, v = load(n)
            p = jnp.exp2(logits(k, n, masked) - lse)
            dp = lax.dot_general(v, do, nt, preferred_element_type=f32)
            ds = (p * (dp - delta) * scale).astype(jnp.bfloat16)
            dk = jnp.dot(ds, q, preferred_element_type=f32)
            dv = jnp.dot(p.astype(jnp.bfloat16), do, preferred_element_type=f32)
            if g == 1:
                dks[at, :] = dk
                dvs[at, :] = dv
            else:
                dks[at, :] += dk
                dvs[at, :] += dv
            return dq + lax.dot_general(k, ds, tn, preferred_element_type=f32)

        dq = lax.fori_loop(0, last, functools.partial(grads, masked=False), jnp.zeros((hd, width), f32))
        dq = grads(last, dq, True).T
        for h in range(group):
            dq_ref[rows, h * hd:(h + 1) * hd] = dq[h * span:(h + 1) * span, :].astype(jnp.bfloat16)

    def place(s, _):
        at = pl.ds(pl.multiple_of(s * span, span), span)
        dk_ref[pl.ds(pl.multiple_of(at_k[s] * span, span), span), :] = dks[at, :].astype(jnp.bfloat16)
        dv_ref[pl.ds(pl.multiple_of(at_v[s] * span, span), span), :] = dvs[at, :].astype(jnp.bfloat16)
        return 0

    def blank(s, _):
        none = jnp.zeros((span, hd), jnp.bfloat16)
        dk_ref[pl.ds(pl.multiple_of(at_k[s] * span, span), span), :] = none
        dv_ref[pl.ds(pl.multiple_of(at_v[s] * span, span), span), :] = none
        return 0

    lax.fori_loop(0, used, place, 0)
    lax.fori_loop(used, spans, blank, 0)


def local(outer, inner, queries, keys, values, grad_out, span_slot):
    rows, hd = keys.shape
    total = rows * outer * inner
    spans = span_slot.shape[0]
    orders = bits_of(outer, inner)
    steps = len(orders[0])
    low = jnp.bfloat16
    vmem, smem = pl.BlockSpec(memory_space=pltpu.VMEM), pl.BlockSpec(memory_space=pltpu.SMEM)
    sems = [pltpu.SemaphoreType.DMA((2, steps)), pltpu.SemaphoreType.DMA((2, steps))]
    whole = jax.ShapeDtypeStruct((total, hd), low)
    block = jax.ShapeDtypeStruct((rows, hd), low)
    keys_all, values_all = pl.pallas_call(
        functools.partial(gather_kernel, orders),
        out_shape=(whole, whole), in_specs=[vmem] * 2, out_specs=(vmem, vmem), scratch_shapes=sems,
        compiler_params=pltpu.CompilerParams(collective_id=0, has_side_effects=True, vmem_limit_bytes=40 * MIB),
    )(keys, values)
    tables = [
        jnp.asarray(np.array([2 * place_of(order, j // 2 // inner, j // 2 % inner) + j % 2 for j in range(spans)], np.int32))
        for order in orders
    ]
    grad_queries, dk, dv = pl.pallas_call(
        functools.partial(attend_kernel, inner, math.gcd(spans, 4)),
        out_shape=(jax.ShapeDtypeStruct(queries.shape, low), whole, whole),
        in_specs=[smem] * 3 + [vmem] * 4, out_specs=(vmem, vmem, vmem),
        scratch_shapes=[pltpu.SMEM((spans,), jnp.int32), pltpu.SMEM((spans,), jnp.int32),
                        pltpu.VMEM((total, hd), low), pltpu.VMEM((total, hd), low),
                        pltpu.VMEM((total, hd), jnp.float32), pltpu.VMEM((total, hd), jnp.float32)],
        compiler_params=pltpu.CompilerParams(vmem_limit_bytes=56 * MIB),
    )(span_slot, *tables, queries, grad_out, keys_all, values_all)
    grad_keys, grad_values = pl.pallas_call(
        functools.partial(scatter_kernel, orders),
        out_shape=(block, block), in_specs=[vmem] * 2, out_specs=(vmem, vmem),
        scratch_shapes=[pltpu.VMEM((total // 2, hd), low), pltpu.VMEM((total // 2, hd), low),
                        pltpu.VMEM((total, hd), low), pltpu.VMEM((total, hd), low)] + sems,
        compiler_params=pltpu.CompilerParams(collective_id=1, has_side_effects=True, vmem_limit_bytes=40 * MIB),
    )(dk, dv)
    return grad_queries, grad_keys, grad_values


def solution(mesh):
    rows = P(("outer", "inner"), None)
    return jax.shard_map(
        functools.partial(local, mesh.shape["outer"], mesh.shape["inner"]),
        mesh=mesh,
        in_specs=(rows, rows, rows, rows, P()),
        out_specs=(rows, rows, rows),
        check_vma=False,
    )
```

time: 359 us -> 78.2 us (0.22)
  waiting for transfers between devices: 258 us -> 0 us
  Pallas kernels: 0 us -> 70.2 us
  matrix products: 60.4 us -> 0 us
  between operations: 13.8 us -> 0.67 us
  local copies, waits for them, and re-layouts: 19 us -> 7.17 us
  other arithmetic: 5.61 us -> 0 us
    reduce_scatter x1 -> x0, waiting for transfers between devices: 146 us -> none  [local(): lax.psum_scatter(all_terms, ('outer', 'inner'), scatter_dimension=0, tile...]
    all_gather x2 -> x0, waiting for transfers between devices: 111 us -> none  [the longest x1 55.7 us: local(): lax.all_gather(values, ('outer', 'inner'), axis=0, tiled=True)]
    pallas_call x0 -> x3, Pallas kernels: none -> 70.2 us  [the longest x1 26.9 us: local(): pl.pallas_call(functools.partial(gather_kernel, orders), out_shape=(whole...]
    dot_general x56 -> x0, matrix products: 60.4 us -> none  [the longest x8 11.2 us: stats_step(): dprobs = jnp.dot(do_rows, v_blk.T, preferred_element_type=jnp.float32)]
    dynamic_update_slice x16 -> x0, local copies, waits for them, and re-layouts: 8.24 us -> none  [joint_step(): return (acc, lax.dynamic_update_slice_in_dim(terms, piece, first, 0))]
    unnamed x0 -> x14, local copies, waits for them, and re-layouts: none -> 7.17 us
  transfers between devices with their start and end apart: 3 -> 0, of which waited for: 3 -> 0; matrix products, arithmetic and copies ran while one was open for 1% -> 0% of each run, Pallas kernels for 0% -> 0%
where the time goes in v1:
time: 78.2 us; the launch traced here: 78 us
  Pallas kernels  70.2 us (90%)
  local copies, waits for them, and re-layouts  7.17 us (9%)
    pallas_call x1, Pallas kernels, local(): pl.pallas_call(functools.partial(gather_kernel, orders), out_shape=(whole...  26.9 us
    pallas_call x1, Pallas kernels, local(): pl.pallas_call(functools.partial(scatter_kernel, orders), out_shape=(bloc...  24.6 us
    pallas_call x1, Pallas kernels, local(): pl.pallas_call(functools.partial(attend_kernel, inner, math.gcd(spans, 4)...  18.8 us
    unnamed x14, local copies, waits for them, and re-layouts  7.17 us

profile of v1, /device:TPU:0, one launch (start us, length us, event | category | flops | bytes accessed | tf_op | source)
XLA Modules:
  0.0 78.0 jit_solution(13383724715275275246)
XLA Ops:
  0.6 0.0 copy-start.4
  0.6 0.7 copy-done.4
  1.4 0.0 copy-start.5
  1.4 0.8 copy-done.5
  2.1 26.9 %shard_map.94 = (bf16[4096,128]{1,0:T(8,128)(2,1)S(1)}, bf16[4096,128]{1,0:T(8,128)(2,1)S(1)}) custom-call(bf16[128,128]{1,0:T(8,128)(2,1)S(1)} %copy-done.4, bf16[128,128]{1,0:T(8,128)(2,1)S(1)} %copy-done.5), custom_call_target="tpu_custom_call" | custom-call | tf_op jit(solution)/shard_map/pallas_call | solution.py:232
  29.0 0.0 copy-start
  29.0 1.0 %copy-done = bf16[4096,128]{1,0:T(8,128)(2,1)} copy-done((bf16[4096,128]{1,0:T(8,128)(2,1)}, bf16[4096,128]{1,0:T(8,128)(2,1)S(1)}, u32[]{:S(2)}) %copy-start) | copy-done | bytes 1048600
  30.0 0.0 copy-start.1
  30.0 1.0 %copy-done.1 = bf16[4096,128]{1,0:T(8,128)(2,1)} copy-done((bf16[4096,128]{1,0:T(8,128)(2,1)}, bf16[4096,128]{1,0:T(8,128)(2,1)S(1)}, u32[]{:S(2)}) %copy-start.1) | copy-done | bytes 1048600
  31.0 18.8 %shard_map.95 = (bf16[128,768]{1,0:T(8,128)(2,1)}, bf16[4096,128]{1,0:T(8,128)(2,1)}, bf16[4096,128]{1,0:T(8,128)(2,1)}) custom-call(s32[64]{0:T(128)} %slots.1, s32[64]{0:T(128)} %constant.4.clone.tab_k, s32[64]{0:T(128)} %constant.5.clone.tab_v, bf16[128,768]{1,0:T(8,128)(2,1)} %q_ref.1, bf16[128,768]{1,0:T(8,128)(2,1)} %do_ref.1, ...), custom_call_target="tpu_custom_call" | custom-call | tf_op jit(solution)/shard_map/pallas_call | solution.py:241
  49.8 0.0 copy-start.2
  49.8 1.2 %copy-done.2 = bf16[4096,128]{1,0:T(8,128)(2,1)S(1)} copy-done((bf16[4096,128]{1,0:T(8,128)(2,1)S(1)}, bf16[4096,128]{1,0:T(8,128)(2,1)}, u32[]{:S(2)}) %copy-start.2) | copy-done | bytes 1048600
  51.0 0.0 copy-start.3
  51.0 1.2 %copy-done.3 = bf16[4096,128]{1,0:T(8,128)(2,1)S(1)} copy-done((bf16[4096,128]{1,0:T(8,128)(2,1)S(1)}, bf16[4096,128]{1,0:T(8,128)(2,1)}, u32[]{:S(2)}) %copy-start.3) | copy-done | bytes 1048600
  52.2 24.6 %shard_map.96 = (bf16[128,128]{1,0:T(8,128)(2,1)S(1)}, bf16[128,128]{1,0:T(8,128)(2,1)S(1)}) custom-call(bf16[4096,128]{1,0:T(8,128)(2,1)S(1)} %copy-done.2, bf16[4096,128]{1,0:T(8,128)(2,1)S(1)} %copy-done.3), custom_call_target="tpu_custom_call" | custom-call | tf_op jit(solution)/shard_map/pallas_call | solution.py:250
  76.8 0.6 copy.12
  77.4 0.6 copy.13
Async XLA Ops:
  0.6 0.8 copy-start.4
  1.4 0.8 copy-start.5
  29.0 1.0 %copy-start = (bf16[4096,128]{1,0:T(8,128)(2,1)}, bf16[4096,128]{1,0:T(8,128)(2,1)S(1)}, u32[]{:S(2)}) copy-start(bf16[4096,128]{1,0:T(8,128)(2,1)S(1)} %get-tuple-element.10.k_ref) | copy-start | bytes 3145732
  30.0 1.0 %copy-start.1 = (bf16[4096,128]{1,0:T(8,128)(2,1)}, bf16[4096,128]{1,0:T(8,128)(2,1)S(1)}, u32[]{:S(2)}) copy-start(bf16[4096,128]{1,0:T(8,128)(2,1)S(1)} %get-tuple-element.11.v_ref) | copy-start | bytes 3145732
  49.8 1.2 %copy-start.2 = (bf16[4096,128]{1,0:T(8,128)(2,1)S(1)}, bf16[4096,128]{1,0:T(8,128)(2,1)}, u32[]{:S(2)}) copy-start(bf16[4096,128]{1,0:T(8,128)(2,1)} %get-tuple-element.13.k_in) | copy-start | bytes 3145732
  51.0 1.2 %copy-start.3 = (bf16[4096,128]{1,0:T(8,128)(2,1)S(1)}, bf16[4096,128]{1,0:T(8,128)(2,1)}, u32[]{:S(2)}) copy-start(bf16[4096,128]{1,0:T(8,128)(2,1)} %get-tuple-element.14.v_in) | copy-start | bytes 3145732

commit v2 on v1

v2 whole, which is shorter than its diff:
```python
import functools
import math

import jax
import jax.numpy as jnp
import numpy as np
from jax import lax
from jax.experimental import pallas as pl
from jax.experimental.pallas import tpu as pltpu
from jax.sharding import PartitionSpec as P

NEG_FILL = -1e30
LOG2E = math.log2(math.e)
MIB = 1024 * 1024
MESH = pl.DeviceIdType.MESH


def bits_of(outer, inner):
    near = [("inner", b) for b in range(inner.bit_length() - 1)]
    chips = [("outer", b) for b in range(1, outer.bit_length() - 1)]
    core = [("outer", 0)]
    return near + chips + core, near[::-1] + chips[::-1] + core


def place_of(order, o, i):
    place = 0
    for at, (axis, b) in enumerate(order):
        place = place + (((o if axis == "outer" else i) // 2**b) % 2) * 2**at
    return place


def partner_of(axis, b, o, i):
    if axis == "outer":
        return (o + (1 - 2 * ((o // 2**b) % 2)) * 2**b, i)
    return (o, i + (1 - 2 * ((i // 2**b) % 2)) * 2**b)


def greet(order, o, i):
    barrier = pltpu.get_barrier_semaphore()
    for axis, b in order:
        pl.semaphore_signal(barrier, inc=1, device_id=partner_of(axis, b, o, i), device_id_type=MESH)
    pl.semaphore_wait(barrier, len(order))


def gather_kernel(orders, k_in, v_in, k_out, v_out, send, recv, own):
    o, i = lax.axis_index("outer"), lax.axis_index("inner")
    rows = k_in.shape[0]
    chain = len(orders[0]) - 1
    near = sum(axis == "inner" for axis, _ in orders[0])
    places = [place_of(order, o, i) for order in orders]
    outs = (k_out, v_out)

    def span_of(place, step):
        size = rows * 2**step
        return pl.ds(pl.multiple_of((place // 2**step) * size, size), size)

    owned = [
        pltpu.make_async_copy((k_in, v_in)[a], outs[a].at[span_of(places[a], 0), :], own.at[a]) for a in (0, 1)
    ]
    for copy in owned:
        copy.start()
    greet(orders[0], o, i)
    copies = {}

    def begin(a, name, part, bit):
        part = outs[a].at[part, :]
        copies[a, name] = pltpu.make_async_remote_copy(
            src_ref=part, dst_ref=part, send_sem=send.at[a, name], recv_sem=recv.at[a, name],
            device_id=partner_of(*bit, o, i), device_id_type=MESH)
        copies[a, name].start()

    for a in (0, 1):
        owned[a].wait()
        begin(a, 0, span_of(places[a], 0), orders[a][0])
    core = orders[0][chain]
    for step in range(chain):
        for a in (0, 1):
            copies[a, step].wait_recv()
            if step + 1 < chain:
                begin(a, step + 1, span_of(places[a], step + 1), orders[a][step + 1])
            if step == near - 1:
                begin(a, chain, span_of(places[a], near), core)
            elif step >= near:
                theirs = places[a] + (1 - 2 * ((places[a] // 2**step) % 2)) * 2**step
                begin(a, chain + 1 + step - near, span_of(theirs, step), core)
    for (_, name), copy in copies.items():
        copy.wait_send()
        if name >= chain:
            copy.wait_recv()


def scatter_kernel(orders, k_in, v_in, k_out, v_out, k_acc, v_acc, k_got, v_got, k_core, v_core, send, recv):
    o, i = lax.axis_index("outer"), lax.axis_index("inner")
    rows = k_out.shape[0]
    chain = len(orders[0]) - 1
    near = sum(axis == "inner" for axis, _ in orders[0])
    greet(orders[0], o, i)
    half = 2**chain
    ins, outs, accs = (k_in, v_in), (k_out, v_out), (k_acc, v_acc)
    gots, cores = (k_got, v_got), (k_core, v_core)
    full = [place_of(order, o, i) for order in orders]
    places = [place % half for place in full]
    sides = [place // half for place in full]
    copies = {}

    def spot(place, step):
        size = rows * 2**step
        return pl.ds(pl.multiple_of((place // 2**step) * size, size), size)

    def inside(place, step, side):
        size = rows * 2**step
        return pl.ds(pl.multiple_of((place // 2**step) * size + side * half * rows, size), size)

    def theirs(a, step):
        return places[a] + (1 - 2 * ((places[a] // 2**step) % 2)) * 2**step

    def begin(a, name, src, dst, bit):
        copies[a, name] = pltpu.make_async_remote_copy(
            src_ref=src, dst_ref=dst, send_sem=send.at[a, name], recv_sem=recv.at[a, name],
            device_id=partner_of(*bit, o, i), device_id_type=MESH)
        copies[a, name].start()

    def forward(a, step):
        size = rows * 2**step
        begin(a, step, accs[a].at[spot(theirs(a, step), step), :], gots[a].at[pl.ds(size, size), :], orders[a][step])

    def pieces(a):
        return [(chain + 1 + step - near, theirs(a, step), step) for step in range(chain - 1, near - 1, -1)] + [
            (chain, places[a], near)]

    def join(a, which):
        name, place, step = pieces(a)[which]
        copies[a, name].wait_recv()
        at = spot(place, step)
        total = ins[a][inside(place, step, sides[a]), :].astype(jnp.float32) + cores[a][at, :].astype(jnp.float32)
        accs[a][at, :] = total.astype(jnp.bfloat16)

    chips = chain - near
    for which in range(chips + 1):
        for a in (0, 1):
            name, place, step = pieces(a)[which]
            begin(a, name, ins[a].at[inside(place, step, 1 - sides[a]), :], cores[a].at[spot(place, step), :],
                  orders[a][chain])
    for a in (0, 1):
        join(a, 0)
        forward(a, chain - 1)
    for which in range(1, chips + 1):
        for a in (0, 1):
            join(a, which)
    for step in range(chain - 1, -1, -1):
        size = rows * 2**step
        for a in (0, 1):
            copies[a, step].wait_recv()

            def add(part, place, at_step):
                lo = (place // 2**at_step) * 2**at_step - (places[a] // 2**step) * 2**step
                got = gots[a][pl.ds(pl.multiple_of(size + lo * rows, rows), rows * 2**at_step), :]
                return accs[a][part, :].astype(jnp.float32) + got.astype(jnp.float32)

            if step:
                first, rest = spot(theirs(a, step - 1), step - 1), spot(places[a], step - 1)
                accs[a][first, :] = add(first, theirs(a, step - 1), step - 1).astype(jnp.bfloat16)
                forward(a, step - 1)
                accs[a][rest, :] = add(rest, places[a], step - 1).astype(jnp.bfloat16)
            else:
                outs[a][...] = add(spot(places[a], 0), places[a], 0).astype(jnp.bfloat16)
    for copy in copies.values():
        copy.wait_send()


def attend_kernel(inner, blk_spans, slots, tab_k, tab_v, q_in, do_in, k_ref, v_ref,
                  dq_ref, dk_ref, dv_ref, at_k, at_v, ks, vs, q_ref, do_ref, sem):
    fetches = [pltpu.make_async_copy(q_in, q_ref, sem.at[0]), pltpu.make_async_copy(do_in, do_ref, sem.at[1])]
    for fetch in fetches:
        fetch.start()
    spans = slots.shape[0]
    span = q_ref.shape[0] // 2
    hd = k_ref.shape[1]
    group = q_ref.shape[1] // hd
    blk = blk_spans * span
    scale = 1.0 / math.sqrt(hd)
    f32 = jnp.float32
    linear = lax.axis_index("outer") * inner + lax.axis_index("inner")

    def note(j, _):
        s = slots[j]
        at_k[s] = tab_k[j] * span
        at_v[s] = tab_v[j] * span
        return 0

    lax.fori_loop(0, spans, note, 0)
    tops = [slots[2 * linear], slots[2 * linear + 1]]
    lasts = [top // blk_spans for top in tops]

    def rows_at(table, s):
        return pl.ds(pl.multiple_of(table[s], span), span)

    nt = (((1,), (1,)), ((), ()))
    tn = (((0,), (0,)), ((), ()))
    width = group * span

    def stack(ref):
        return jnp.concatenate(
            [ref[g * span:(g + 1) * span, h * hd:(h + 1) * hd] for g in (0, 1) for h in range(group)], axis=0)

    for fetch in fetches:
        fetch.wait()
    q, do = stack(q_ref), stack(do_ref)
    lane = lax.broadcasted_iota(jnp.int32, (1, 2 * width), 1)
    q_pos = lane % span + jnp.where(lane < width, tops[0], tops[1]) * span
    low = lax.broadcasted_iota(jnp.int32, (blk, 1), 0)

    def logits(k, n, first, masked):
        t = lax.dot_general(k, q[first:], nt, preferred_element_type=f32) * (scale * LOG2E)
        if masked:
            t = jnp.where(low + n * blk <= q_pos[:, first:], t, NEG_FILL)
        return t

    def stats(n, carry, first, masked):
        top, total, weighted = carry
        at = pl.ds(pl.multiple_of(n * blk, blk), blk)
        spots = [(n * blk_spans + j) for j in range(blk_spans)]
        k = jnp.concatenate([k_ref[rows_at(at_k, s), :] for s in spots], axis=0)
        v = jnp.concatenate([v_ref[rows_at(at_v, s), :] for s in spots], axis=0)
        ks[at, :] = k
        vs[at, :] = v
        t = logits(k, n, first, masked)
        dp = lax.dot_general(v, do[first:], nt, preferred_element_type=f32)
        new = jnp.maximum(top, jnp.max(t, axis=0, keepdims=True))
        shrink = jnp.exp2(top - new)
        e = jnp.exp2(t - new)
        return (new, total * shrink + jnp.sum(e, axis=0, keepdims=True),
                weighted * shrink + jnp.sum(e * dp, axis=0, keepdims=True))

    def sweep(step, carry, narrow):
        carry = lax.fori_loop(0, lasts[0], functools.partial(step, first=0, masked=False), carry)
        carry = step(lasts[0], carry, 0, True)
        late = narrow(carry)
        late = lax.fori_loop(lasts[0] + 1, lasts[1], functools.partial(step, first=width, masked=False), late)
        return carry, step(lasts[1], late, width, True)

    start = (jnp.full((1, 2 * width), NEG_FILL, f32), jnp.zeros((1, 2 * width), f32), jnp.zeros((1, 2 * width), f32))
    early, late = sweep(stats, start, lambda carry: tuple(x[:, width:] for x in carry))
    top, total, weighted = [jnp.concatenate([x[:, :width], y], axis=1) for x, y in zip(early, late)]
    lse = top + jnp.log2(total)
    delta = weighted / total

    def grads(n, dq, first, masked):
        at = pl.ds(pl.multiple_of(n * blk, blk), blk)
        k, v = ks[at, :], vs[at, :]
        p = jnp.exp2(logits(k, n, first, masked) - lse[:, first:])
        dp = lax.dot_general(v, do[first:], nt, preferred_element_type=f32)
        ds = (p * (dp - delta[:, first:]) * scale).astype(jnp.bfloat16)
        dk = jnp.dot(ds, q[first:], preferred_element_type=f32).astype(jnp.bfloat16)
        dv = jnp.dot(p.astype(jnp.bfloat16), do[first:], preferred_element_type=f32).astype(jnp.bfloat16)
        for j in range(blk_spans):
            s = n * blk_spans + j
            dk_ref[rows_at(at_k, s), :] = dk[j * span:(j + 1) * span]
            dv_ref[rows_at(at_v, s), :] = dv[j * span:(j + 1) * span]
        return dq + lax.dot_general(k, ds, tn, preferred_element_type=f32)

    early, late = sweep(grads, jnp.zeros((hd, 2 * width), f32), lambda dq: dq[:, width:])
    dq = jnp.concatenate([early[:, :width], late], axis=1).T
    for g in (0, 1):
        for h in range(group):
            at = (g * group + h) * span
            dq_ref[g * span:(g + 1) * span, h * hd:(h + 1) * hd] = dq[at:at + span].astype(jnp.bfloat16)

    def blank(s, _):
        none = jnp.zeros((span, hd), jnp.bfloat16)
        dk_ref[rows_at(at_k, s), :] = none
        dv_ref[rows_at(at_v, s), :] = none
        return 0

    lax.fori_loop((lasts[1] + 1) * blk_spans, spans, blank, 0)


def local(outer, inner, queries, keys, values, grad_out, span_slot):
    rows, hd = keys.shape
    total = rows * outer * inner
    spans = span_slot.shape[0]
    orders = bits_of(outer, inner)
    steps = len(orders[0])
    low = jnp.bfloat16
    vmem, smem = pl.BlockSpec(memory_space=pltpu.VMEM), pl.BlockSpec(memory_space=pltpu.SMEM)
    moves = steps + outer.bit_length() - 2
    hbm = pl.BlockSpec(memory_space=pltpu.HBM)
    sems = [pltpu.SemaphoreType.DMA((2, moves)), pltpu.SemaphoreType.DMA((2, moves))]
    unit = total * hd
    whole = jax.ShapeDtypeStruct((total, hd), low)
    block = jax.ShapeDtypeStruct((rows, hd), low)
    keys_all, values_all = pl.pallas_call(
        functools.partial(gather_kernel, orders),
        out_shape=(whole, whole), in_specs=[hbm] * 2, out_specs=(vmem, vmem),
        scratch_shapes=sems + [pltpu.SemaphoreType.DMA((2,))],
        compiler_params=pltpu.CompilerParams(
            collective_id=0, has_side_effects=True, vmem_limit_bytes=4 * unit + 4 * MIB),
    )(keys, values)
    tables = [
        jnp.asarray(np.array([2 * place_of(order, j // 2 // inner, j // 2 % inner) + j % 2 for j in range(spans)], np.int32))
        for order in orders
    ]
    grad_queries, dk, dv = pl.pallas_call(
        functools.partial(attend_kernel, inner, math.gcd(spans, 4)),
        out_shape=(jax.ShapeDtypeStruct(queries.shape, low), whole, whole),
        in_specs=[smem] * 3 + [hbm] * 2 + [vmem] * 2, out_specs=(vmem, vmem, vmem),
        scratch_shapes=[pltpu.SMEM((spans,), jnp.int32), pltpu.SMEM((spans,), jnp.int32),
                        pltpu.VMEM((total, hd), low), pltpu.VMEM((total, hd), low),
                        pltpu.VMEM(queries.shape, low), pltpu.VMEM(queries.shape, low),
                        pltpu.SemaphoreType.DMA((2,))],
        compiler_params=pltpu.CompilerParams(vmem_limit_bytes=12 * unit + 12 * MIB),
    )(span_slot, *tables, queries, grad_out, keys_all, values_all)
    grad_keys, grad_values = pl.pallas_call(
        functools.partial(scatter_kernel, orders),
        out_shape=(block, block), in_specs=[vmem] * 2, out_specs=(vmem, vmem),
        scratch_shapes=[pltpu.VMEM((total // 2, hd), low), pltpu.VMEM((total // 2, hd), low),
                        pltpu.VMEM((total // 2, hd), low), pltpu.VMEM((total // 2, hd), low),
                        pltpu.VMEM((total // 2, hd), low), pltpu.VMEM((total // 2, hd), low)] + sems,
        compiler_params=pltpu.CompilerParams(
            collective_id=1, has_side_effects=True, vmem_limit_bytes=10 * unit + 4 * MIB),
    )(dk, dv)
    return grad_queries, grad_keys, grad_values


def solution(mesh):
    rows = P(("outer", "inner"), None)
    return jax.shard_map(
        functools.partial(local, mesh.shape["outer"], mesh.shape["inner"]),
        mesh=mesh,
        in_specs=(rows, rows, rows, rows, P()),
        out_specs=(rows, rows, rows),
        check_vma=False,
    )
```

time: 78.2 us -> 69 us (0.88); the launches traced: 78 us -> 68 us
  Pallas kernels: 70.2 us -> 62.1 us
  local copies, waits for them, and re-layouts: 7.17 us -> 5.26 us
    pallas_call x1, Pallas kernels: 18.8 us -> 12.9 us  [local(): pl.pallas_call(functools.partial(attend_kernel, inner, math.gcd(spans, 4)...]
    pallas_call x1, Pallas kernels: 26.9 us -> 24.1 us  [local(): pl.pallas_call(functools.partial(gather_kernel, orders), out_shape=(whole...]
    unnamed x14 -> x16, local copies, waits for them, and re-layouts: 7.17 us -> 5.26 us
where the time goes in v2:
time: 69 us; the launch traced here: 68 us
  Pallas kernels  62.1 us (90%)
  local copies, waits for them, and re-layouts  5.26 us (8%)
    pallas_call x1, Pallas kernels, local(): pl.pallas_call(functools.partial(scatter_kernel, orders), out_shape=(bloc...  25.1 us
    pallas_call x1, Pallas kernels, local(): pl.pallas_call(functools.partial(gather_kernel, orders), out_shape=(whole...  24.1 us
    pallas_call x1, Pallas kernels, local(): pl.pallas_call(functools.partial(attend_kernel, inner, math.gcd(spans, 4)...  12.9 us
    unnamed x16, local copies, waits for them, and re-layouts  5.26 us

profile of v2, /device:TPU:0, one launch (start us, length us, event | category | flops | bytes accessed | tf_op | source)
XLA Modules:
  0.0 68.0 jit_solution(15481198307974157033)
XLA Ops:
  0.6 0.0 copy-start.2
  0.6 0.7 %copy-done.2 = bf16[128,128]{1,0:T(8,128)(2,1)S(1)} copy-done((bf16[128,128]{1,0:T(8,128)(2,1)S(1)}, bf16[128,128]{1,0:T(8,128)(2,1)}, u32[]{:S(2)}) %copy-start.2) | copy-done | bytes 32792
  1.4 0.0 copy-start.3
  1.4 0.8 %copy-done.3 = bf16[128,128]{1,0:T(8,128)(2,1)S(1)} copy-done((bf16[128,128]{1,0:T(8,128)(2,1)S(1)}, bf16[128,128]{1,0:T(8,128)(2,1)}, u32[]{:S(2)}) %copy-start.3) | copy-done | bytes 32792
  2.1 24.1 %shard_map.94 = (bf16[4096,128]{1,0:T(8,128)(2,1)S(1)}, bf16[4096,128]{1,0:T(8,128)(2,1)S(1)}) custom-call(bf16[128,128]{1,0:T(8,128)(2,1)S(1)} %copy-done.2, bf16[128,128]{1,0:T(8,128)(2,1)S(1)} %copy-done.3), custom_call_target="tpu_custom_call" | custom-call | tf_op jit(solution)/shard_map/pallas_call | solution.py:292
  26.2 0.0 copy-start.4
  26.2 0.0 copy-start.5
  26.2 0.0 copy-start.6
  26.3 0.6 copy-done.4
  26.9 0.0 copy-done.5
  26.9 0.0 copy-done.6
  26.9 0.0 copy-start
  26.9 0.9 %copy-done = bf16[128,768]{1,0:T(8,128)(2,1)S(1)} copy-done((bf16[128,768]{1,0:T(8,128)(2,1)S(1)}, bf16[128,768]{1,0:T(8,128)(2,1)}, u32[]{:S(2)}) %copy-start) | copy-done | bytes 196632
  27.8 0.0 copy-start.1
  27.8 0.9 %copy-done.1 = bf16[128,768]{1,0:T(8,128)(2,1)S(1)} copy-done((bf16[128,768]{1,0:T(8,128)(2,1)S(1)}, bf16[128,768]{1,0:T(8,128)(2,1)}, u32[]{:S(2)}) %copy-start.1) | copy-done | bytes 196632
  28.8 12.9 %shard_map.95 = (bf16[128,768]{1,0:T(8,128)(2,1)}, bf16[4096,128]{1,0:T(8,128)(2,1)S(1)}, bf16[4096,128]{1,0:T(8,128)(2,1)S(1)}) custom-call(s32[64]{0:T(128)S(1)} %copy-done.4, s32[64]{0:T(128)S(1)} %copy-done.6, s32[64]{0:T(128)S(1)} %copy-done.5, bf16[128,768]{1,0:T(8,128)(2,1)S(1)} %copy-done, bf16[128,768]{1,0:T(8,128)(2,1)S(1)} %copy-done.1, ...), custom_call_target="tpu_custom_call" | custom-call | tf_op jit(solution)/shard_map/pallas_call | solution.py:303
  41.7 25.1 %shard_map.96 = (bf16[128,128]{1,0:T(8,128)(2,1)S(1)}, bf16[128,128]{1,0:T(8,128)(2,1)S(1)}) custom-call(bf16[4096,128]{1,0:T(8,128)(2,1)S(1)} %get-tuple-element.13.k_in, bf16[4096,128]{1,0:T(8,128)(2,1)S(1)} %get-tuple-element.14.v_in), custom_call_target="tpu_custom_call" | custom-call | tf_op jit(solution)/shard_map/pallas_call | solution.py:313
  66.8 0.6 copy.12
  67.4 0.6 copy.13
Async XLA Ops:
  0.6 0.8 %copy-start.2 = (bf16[128,128]{1,0:T(8,128)(2,1)S(1)}, bf16[128,128]{1,0:T(8,128)(2,1)}, u32[]{:S(2)}) copy-start(bf16[128,128]{1,0:T(8,128)(2,1)} %k_in.1) | copy-start | bytes 98308
  1.4 0.8 %copy-start.3 = (bf16[128,128]{1,0:T(8,128)(2,1)S(1)}, bf16[128,128]{1,0:T(8,128)(2,1)}, u32[]{:S(2)}) copy-start(bf16[128,128]{1,0:T(8,128)(2,1)} %v_in.1) | copy-start | bytes 98308
  26.2 0.7 copy-start.4
  26.2 0.7 copy-start.5
  26.2 0.7 copy-start.6
  26.9 0.9 %copy-start = (bf16[128,768]{1,0:T(8,128)(2,1)S(1)}, bf16[128,768]{1,0:T(8,128)(2,1)}, u32[]{:S(2)}) copy-start(bf16[128,768]{1,0:T(8,128)(2,1)} %q_in.1) | copy-start | bytes 589828
  27.8 0.9 %copy-start.1 = (bf16[128,768]{1,0:T(8,128)(2,1)S(1)}, bf16[128,768]{1,0:T(8,128)(2,1)}, u32[]{:S(2)}) copy-start(bf16[128,768]{1,0:T(8,128)(2,1)} %do_in.1) | copy-start | bytes 589828
